TPU v7x, 32 devices: a whole 2x2x4 slice. The times are simulated.
32 devices in a mesh: groups: 2 (over y), dp: 1, expert: 16 (over z, x, core).
Axes of the slice: x: 2, y: 2, z: 4, core: 2. Of those that a mesh axis runs over, the one named last changes fastest.
Arguments:
- inner: bfloat16 [4096, 8, 384], P(('groups', 'dp', 'expert')), parts along dimension 0, may hold values from -0.59765625 to 0.59765625
- upstream: bfloat16 [4096, 2048], P(('groups', 'dp', 'expert')), parts along dimension 0, may hold values from -6 to 6
- routes: int32 [4096, 8], P(('groups', 'dp', 'expert')), parts along dimension 0, may hold values from 0 to 15, all different within a row; in each aligned block of 128 rows (0 to 127, 128 to 255, ...) at most 96 rows name the same one
- gates: float32 [4096, 8], P(('groups', 'dp', 'expert')), parts along dimension 0, may hold values from 0.2 to 1
- lengths: int32 [4], P('groups'), parts along dimension 0, may hold values from 1 to 1536, 2048 in all
- advantages: float32 [4], P('groups'), parts along dimension 0, may hold values from -4 to 4
- down_weight: bfloat16 [16, 2048, 384], P('expert', 'dp'), may hold values from -0.125 to 0.125
Outputs:
- grad_inner: bfloat16 [4096, 8, 384], P(('groups', 'dp', 'expert')), parts along dimension 0
- grad_down: bfloat16 [32, 2048, 384], P(('groups', 'expert'), 'dp'), parts along dimension 0
There are 2 independent parts, one for each index of `groups`. A program takes and returns all parts, laid end to end along the dimension named above; an argument that names none is the same for every part. Nothing has to cross between parts.
Inputs may be any that keep to these rules, and one draw needn't show every extreme that they name: `routes`: within the rows of one device no expert is named more than 96 times, a bound that some block reaches; the ids of one token differ. The lengths sum to 2048; none is longer than 1536.
All inputs are finite; a program needn't handle non-finite values.
Results may differ from a plain program's by a relative error of at most 0.005.
Values may be sent and summed in bfloat16 or wider, within the bound.
A program may use at most 128 MiB of HBM per device.

v0:
```python
import jax
import jax.numpy as jnp
from jax import lax
from jax.sharding import PartitionSpec as P


def slot_layout(routes, experts_all, capacity):
    flat_route = routes.reshape(-1)
    chosen = (flat_route[:, None] == jnp.arange(experts_all, dtype=jnp.int32)[None, :]).astype(
        jnp.int32
    )
    before = jnp.cumsum(chosen, axis=0) - chosen
    rank_in = jnp.sum(before * chosen, axis=1)
    return flat_route * capacity + rank_in


def shards(inner, upstream, routes, gates, lengths, advantages, down_weight):
    tok_rows, top_count = routes.shape
    width = upstream.shape[1]
    hidden = inner.shape[2]
    expert_devs = lax.axis_size("expert")
    local_experts = down_weight.shape[0]
    experts_all = local_experts * expert_devs
    capacity = min(tok_rows, max(2, 3 * tok_rows * top_count // (2 * experts_all)))
    first_row = (lax.axis_index("dp") * expert_devs + lax.axis_index("expert")) * tok_rows
    position = first_row + jnp.arange(tok_rows, dtype=jnp.int32)
    ends = jnp.cumsum(lengths)
    seq_index = jnp.sum((position[:, None] >= ends[None, :]).astype(jnp.int32), axis=1)
    member = seq_index[:, None] == jnp.arange(lengths.shape[0], dtype=jnp.int32)[None, :]
    token_adv = jnp.sum(jnp.where(member, advantages[None, :], 0.0), axis=1)
    factor = gates * token_adv[:, None]
    weighted = (factor[:, :, None] * upstream[:, None, :].astype(jnp.float32)).astype(jnp.bfloat16)
    target = slot_layout(routes, experts_all, capacity)
    buffer_rows = experts_all * capacity
    block_rows = local_experts * capacity
    flat_weighted = weighted.reshape(-1, width)
    flat_inner = inner.reshape(-1, hidden)
    send_h = jnp.zeros((buffer_rows, hidden), jnp.bfloat16).at[target].set(flat_inner)
    send_w = jnp.zeros((buffer_rows, width), jnp.bfloat16).at[target].set(flat_weighted)
    recv_w, recv_h = (
        lax.all_to_all(
            send_w.reshape(expert_devs, block_rows, width),
            "expert",
            split_axis=0,
            concat_axis=0,
            tiled=True,
        ),
        lax.all_to_all(
            send_h.reshape(expert_devs, block_rows, hidden),
            "expert",
            split_axis=0,
            concat_axis=0,
            tiled=True,
        ),
    )
    recv_w = recv_w.reshape(expert_devs, local_experts, capacity, width)
    recv_h = recv_h.reshape(expert_devs, local_experts, capacity, hidden)
    columns = recv_w
    back_grad = jnp.einsum(
        "sect,eth->sech",
        columns,
        lax.all_gather(down_weight, "dp", axis=1, tiled=True),
        preferred_element_type=jnp.float32,
    )
    returned = lax.all_to_all(
        back_grad.astype(jnp.bfloat16).reshape(expert_devs, block_rows, hidden),
        "expert",
        split_axis=0,
        concat_axis=0,
        tiled=True,
    )
    grad_slots = returned.reshape(buffer_rows, hidden)
    columns = recv_w
    shares = lax.psum_scatter(
        jnp.einsum("secd,sech->deh", columns, recv_h, preferred_element_type=jnp.float32),
        "dp",
        scatter_dimension=0,
        tiled=True,
    )
    grad_down = jnp.transpose(shares, (1, 0, 2)).astype(jnp.bfloat16)
    grad_inner = grad_slots[target].reshape(tok_rows, top_count, hidden)
    return (grad_inner, grad_down)


def solution(mesh):
    return jax.shard_map(
        shards,
        mesh=mesh,
        in_specs=(
            P(("groups", "dp", "expert"), None, None),
            P(("groups", "dp", "expert"), None),
            P(("groups", "dp", "expert"), None),
            P(("groups", "dp", "expert"), None),
            P("groups"),
            P("groups"),
            P("expert", "dp", None),
        ),
        out_specs=(P(("groups", "dp", "expert"), None, None), P(("groups", "expert"), "dp", None)),
        check_vma=False,
    )
```

profile of v0, /device:TPU:1, one launch (start us, length us, event | category | flops | bytes accessed | tf_op | source)
XLA Modules:
  0.0 235.8 jit_solution(4834132904425478648)
XLA Ops:
  0.6 0.0 copy-start
  0.6 0.9 copy.20
  1.6 0.1 eq.42
  1.6 0.1 eq.38
  1.7 0.7 broadcast_multiply_fusion.1
  2.4 4.5 %reduce-window.18 = s32[16,8,128]{2,1,0:T(8,128)S(1)} reduce-window(s32[16,8,128]{2,1,0:T(8,128)S(1)} %fusion.18, s32[]{:T(128)} %constant.13.clone.1), window={size=1x1x128 pad=0_0x0_0x127_0}, to_apply=%region_0.0 | reduce-window | flops 2080768 | bytes 131076 | tf_op jit(solution)/shard_map/reduce-window
  7.0 0.1 slice.10
  7.0 0.1 copy.22
  7.2 0.1 copy.23
  7.3 0.1 broadcast_add_fusion
  7.4 0.1 copy.19
  7.5 0.1 mul.51
  7.6 1.1 convert_element_type.47
  8.7 0.8 reduce-window.20
  9.6 0.1 fusion.19
  9.6 0.7 fusion.20
  10.4 0.7 broadcast_multiply_fusion
  11.1 0.1 copy.24
  11.2 0.1 mul.56
  11.3 10.6 %scatter_custom_fusion = bf16[1536,2048]{1,0:T(8,128)(2,1)} fusion(s32[1024]{0:T(1024)S(1)} %bitcast.59, f32[128,2048]{1,0:T(8,128)S(1)} %convert_element_type.47, f32[1024]{0:T(1024)S(1)} %mul.56, bf16[]{:T(256)} %constant.10.clone.1), kind=kCustom, calls=%fused_computation.5 | custom fusion | flops 4194304 | bytes 7344130 | tf_op jit(solution)/shard_map/scatter | solution.py:39
  21.9 7.5 %all-to-all-start = ((bf16[16,96,2048]{2,1,0:T(8,128)(2,1)}), bf16[16,96,2048]{2,1,0:T(8,128)(2,1)}, u32[]{:S(2)}, u32[]{:S(2)}) async-start(bf16[16,96,2048]{2,1,0:T(8,128)(2,1)} %bitcast.54), calls=%async_computation | async-start | bytes 12582912 | tf_op jit(solution)/shard_map/all_to_all | solution.py:41
  29.4 6.1 %scatter_custom_fusion.1 = bf16[1536,384]{1,0:T(8,128)(2,1)} fusion(s32[1024]{0:T(1024)S(1)} %bitcast.60, bf16[128,8,384]{2,1,0:T(8,128)(2,1)S(1)} %copy-done.2, bf16[]{:T(256)} %constant.10.clone.1), kind=kCustom, calls=%fused_computation.14 | custom fusion | bytes 1966082 | tf_op jit(solution)/shard_map/scatter | solution.py:38
  35.5 108.5 %all-to-all-done = bf16[16,96,2048]{2,1,0:T(8,128)(2,1)} async-done(((bf16[16,96,2048]{2,1,0:T(8,128)(2,1)}), bf16[16,96,2048]{2,1,0:T(8,128)(2,1)}, u32[]{:S(2)}, u32[]{:S(2)}) %all-to-all-start) | async-done | bytes 6291488 | tf_op jit(solution)/shard_map/all_to_all | solution.py:41
  144.0 27.7 %all-to-all-start.2 = ((bf16[16,96,384]{2,1,0:T(8,128)(2,1)}), bf16[16,96,384]{2,1,0:T(8,128)(2,1)S(1)}, u32[]{:S(2)}, u32[]{:S(2)}) async-start(bf16[16,96,384]{2,1,0:T(8,128)(2,1)} %bitcast.13), calls=%async_computation.2 | async-start | bytes 2359296 | tf_op jit(solution)/shard_map/all_to_all | solution.py:48
  171.7 7.4 %fusion.9 = bf16[16,96,384]{2,1,0:T(8,128)(2,1)} fusion(bf16[16,96,2048]{2,1,0:T(8,128)(2,1)} %all-to-all-done, bf16[1,2048,384]{2,1,0:T(8,128)(2,1)S(1)} %copy-done), kind=kOutput, calls=%fused_computation.13 | convolution fusion | flops 2416508928 | bytes 9043968 | tf_op jit(solution)/shard_map/sect,eth->sech/dot_general | solution.py:59
  179.1 18.1 %all-to-all-done.2 = bf16[16,96,384]{2,1,0:T(8,128)(2,1)S(1)} async-done(((bf16[16,96,384]{2,1,0:T(8,128)(2,1)}), bf16[16,96,384]{2,1,0:T(8,128)(2,1)S(1)}, u32[]{:S(2)}, u32[]{:S(2)}) %all-to-all-start.2) | async-done | bytes 1179680 | tf_op jit(solution)/shard_map/all_to_all | solution.py:48
  197.2 1.0 copy-done.1
  198.2 7.1 %all-to-all-start.1 = ((bf16[16,96,384]{2,1,0:T(8,128)(2,1)}), bf16[16,96,384]{2,1,0:T(8,128)(2,1)S(1)}, u32[]{:S(2)}, u32[]{:S(2)}) async-start(bf16[16,96,384]{2,1,0:T(8,128)(2,1)} %fusion.9), calls=%async_computation.1 | async-start | bytes 2359296 | tf_op jit(solution)/shard_map/all_to_all | solution.py:65
  205.3 7.0 %fusion.6 = bf16[1,2048,384]{1,2,0:T(8,128)(2,1)} fusion(bf16[16,96,384]{2,1,0:T(8,128)(2,1)} %copy-done.1, bf16[16,96,2048]{2,1,0:T(8,128)(2,1)} %all-to-all-done), kind=kOutput, calls=%fused_computation.10 | convolution fusion | flops 2416705536 | bytes 9043968 | tf_op jit(solution)/shard_map/secd,sech->deh/dot_general | solution.py:75
  212.3 2.6 %copy.25 = bf16[1,2048,384]{2,1,0:T(8,128)(2,1)} copy(bf16[1,2048,384]{1,2,0:T(8,128)(2,1)} %fusion.6) | data formatting | bytes 3145728
  214.9 16.0 %all-to-all-done.1 = bf16[16,96,384]{2,1,0:T(8,128)(2,1)S(1)} async-done(((bf16[16,96,384]{2,1,0:T(8,128)(2,1)}), bf16[16,96,384]{2,1,0:T(8,128)(2,1)S(1)}, u32[]{:S(2)}, u32[]{:S(2)}) %all-to-all-start.1) | async-done | bytes 1179680 | tf_op jit(solution)/shard_map/all_to_all | solution.py:65
  230.8 5.0 %gather_fusion = bf16[1024,384]{1,0:T(8,128)(2,1)} fusion(bf16[1536,384]{1,0:T(8,128)(2,1)S(1)} %bitcast.53, s32[1024]{0:T(1024)S(1)} %broadcast_clamp_fusion), kind=kCustom, calls=%fused_computation | custom fusion | bytes 1576960 | tf_op jit(solution)/shard_map/gather | solution.py:81
  (11 shorter events, 0.1 us)
Async XLA Ops:
  0.6 171.1 %copy-start = (bf16[1,2048,384]{2,1,0:T(8,128)(2,1)S(1)}, bf16[1,2048,384]{2,1,0:T(8,128)(2,1)}, u32[]{:S(2)}) copy-start(bf16[1,2048,384]{2,1,0:T(8,128)(2,1)} %param.13) | copy-start | bytes 4718596
  21.9 7.5 %copy-start.2 = (bf16[128,8,384]{2,1,0:T(8,128)(2,1)S(1)}, bf16[128,8,384]{2,1,0:T(8,128)(2,1)}, u32[]{:S(2)}) copy-start(bf16[128,8,384]{2,1,0:T(8,128)(2,1)} %param.7) | copy-start | bytes 2359300
  21.9 122.1 %all-to-all-start = ((bf16[16,96,2048]{2,1,0:T(8,128)(2,1)}), bf16[16,96,2048]{2,1,0:T(8,128)(2,1)}, u32[]{:S(2)}, u32[]{:S(2)}) async-start(bf16[16,96,2048]{2,1,0:T(8,128)(2,1)} %bitcast.54), calls=%async_computation | async-start | bytes 12582912 | tf_op jit(solution)/shard_map/all_to_all | solution.py:41
  144.0 53.2 %all-to-all-start.2 = ((bf16[16,96,384]{2,1,0:T(8,128)(2,1)}), bf16[16,96,384]{2,1,0:T(8,128)(2,1)S(1)}, u32[]{:S(2)}, u32[]{:S(2)}) async-start(bf16[16,96,384]{2,1,0:T(8,128)(2,1)} %bitcast.13), calls=%async_computation.2 | async-start | bytes 2359296 | tf_op jit(solution)/shard_map/all_to_all | solution.py:48
  197.2 1.0 copy-start.1
  198.2 32.6 %all-to-all-start.1 = ((bf16[16,96,384]{2,1,0:T(8,128)(2,1)}), bf16[16,96,384]{2,1,0:T(8,128)(2,1)S(1)}, u32[]{:S(2)}, u32[]{:S(2)}) async-start(bf16[16,96,384]{2,1,0:T(8,128)(2,1)} %fusion.9), calls=%async_computation.1 | async-start | bytes 2359296 | tf_op jit(solution)/shard_map/all_to_all | solution.py:65
where the time goes:
time: 238 us; the launch traced here: 236 us
  waiting for transfers between devices  143 us (60%)
  starting transfers between devices  42.3 us (18%)
  other arithmetic  19.5 us (8%)
  local copies, waits for them, and re-layouts  16.5 us (7%)
  matrix products  14.3 us (6%)
    all_to_all x1, waiting for transfers between devices, shards(): lax.all_to_all(send_w.reshape(expert_devs, block_rows, width), 'expert',...  108 us
    all_to_all x1, starting transfers between devices, shards(): lax.all_to_all(send_h.reshape(expert_devs, block_rows, hidden), 'expert',...  27.7 us
    all_to_all x1, waiting for transfers between devices, shards(): lax.all_to_all(send_h.reshape(expert_devs, block_rows, hidden), 'expert',...  18.1 us
    all_to_all x1, waiting for transfers between devices, shards(): lax.all_to_all(back_grad.astype(jnp.bfloat16).reshape(expert_devs, block_...  16 us
    scatter x1, other arithmetic, shards(): jnp.zeros((buffer_rows, width), jnp.bfloat16).at[target].set(flat_weighted)  10.6 us
    all_to_all x1, starting transfers between devices, shards(): lax.all_to_all(send_w.reshape(expert_devs, block_rows, width), 'expert',...  7.45 us
    dot_general x1, matrix products, shards(): jnp.einsum('sect,eth->sech', columns, lax.all_gather(down_weight, 'dp', a...  7.35 us
    all_to_all x1, starting transfers between devices, shards(): lax.all_to_all(back_grad.astype(jnp.bfloat16).reshape(expert_devs, block_...  7.13 us
  transfers between devices with their start and end apart: 3, of which 3 were waited for; matrix products, arithmetic and copies ran while one was open for 10% of the time, Pallas kernels for 0%

commit v1 on v0

--- a/solution.py
+++ b/solution.py
@@ -1,6 +1,10 @@
+import functools
+
 import jax
 import jax.numpy as jnp
 from jax import lax
+from jax.experimental import pallas as pl
+from jax.experimental.pallas import tpu as pltpu
 from jax.sharding import PartitionSpec as P
 
 
@@ -82,9 +86,365 @@
     return (grad_inner, grad_down)
 
 
+MESH = pl.DeviceIdType.MESH
+CHUNKS = 2
+
+
+def kernel(
+    devs,
+    cap,
+    seqs,
+    routes_t,
+    gates_t,
+    routes_row,
+    lengths,
+    advantages,
+    inner,
+    upstream,
+    down,
+    grad_inner,
+    grad_down,
+    up_all,
+    meta_out,
+    meta_in,
+    inner_out,
+    inner_in,
+    ret_out,
+    ret_in,
+    weighted,
+    total,
+    target_row,
+    target_col,
+    own_sem,
+    up_send,
+    up_recv,
+    meta_send,
+    meta_recv,
+    inner_send,
+    inner_recv,
+    ret_send,
+    ret_recv,
+):
+    top, tok = routes_t.shape
+    slots = top * tok
+    hidden = down.shape[1]
+    depth = devs // 4
+    chips = devs // 2
+    me = lax.axis_index("expert")
+    core = lax.rem(me, 2)
+    chip = lax.div(me, 2)
+    col = lax.rem(chip, 2)
+    z = lax.div(chip, 2)
+    rows = tok // CHUNKS
+    f32, bf16, i32 = jnp.float32, jnp.bfloat16, jnp.int32
+
+    def iota(shape, axis):
+        return lax.broadcasted_iota(i32, shape, axis)
+
+    def device(zs, xs, cs):
+        return (zs * 2 + xs) * 2 + cs
+
+    own = pltpu.make_async_copy(upstream, up_all.at[me], own_sem)
+    own.start()
+    barrier = pltpu.get_barrier_semaphore()
+
+    @pl.loop(1, devs)
+    def _(i):
+        peer = lax.rem(me + i, devs)
+        pl.semaphore_signal(barrier, inc=1, device_id={"expert": peer}, device_id_type=MESH)
+
+    routed = routes_t[...]
+    position = me * tok + iota((1, tok), 1)
+    token_adv = jnp.zeros((1, tok), f32)
+    first = jnp.int32(0)
+    for s in range(seqs):
+        last = first + lengths[s]
+        held = (position >= first) & (position < last)
+        token_adv = jnp.where(held, advantages[s], token_adv)
+        first = last
+    factor = gates_t[...] * token_adv
+    named, factors = [], []
+    for e in range(devs):
+        hit = routed == e
+        named.append(jnp.sum(jnp.where(hit, 1.0, 0.0), axis=0, keepdims=True))
+        factors.append(jnp.sum(jnp.where(hit, factor, 0.0), axis=0, keepdims=True))
+    chosen = jnp.concatenate(named, axis=0)
+    earlier = jnp.where(iota((tok, tok), 0) < iota((tok, tok), 1), 1.0, 0.0).astype(bf16)
+    rank = jnp.dot(chosen.astype(bf16), earlier, preferred_element_type=f32)
+    listed = jnp.where(chosen > 0.5, rank, -1000.0)
+    line = iota((8, tok), 0)
+    for e in range(devs):
+        meta_out[e] = jnp.where(
+            line == 0, factors[e], jnp.where(line == 1, listed[e : e + 1], 0.0)
+        )
+    lane, row = iota((tok, slots), 1), iota((tok, slots), 0)
+    spread = jnp.where((lane >= row * top) & (lane < (row + 1) * top), 1.0, 0.0).astype(bf16)
+    by_slot = jnp.dot(rank.astype(bf16), spread, preferred_element_type=f32)
+    which = iota((devs, slots), 0)
+    start_of = (which * cap).astype(f32)
+    aim = jnp.sum(
+        jnp.where(which == routes_row[...], by_slot + start_of, 0.0), axis=0, keepdims=True
+    )
+    aim8 = jnp.broadcast_to(aim, (8, slots))
+    target_row[...] = aim8.astype(i32)
+    target_col[...] = jnp.transpose(aim8).astype(i32)
+
+    own.wait()
+    pl.semaphore_wait(barrier, devs - 1)
+
+    def up_copy(source, part, zs, kind, peer):
+        block = up_all.at[source, pl.ds(part * rows, rows)]
+        return pltpu.make_async_remote_copy(
+            src_ref=block,
+            dst_ref=block,
+            send_sem=up_send.at[zs, kind, part],
+            recv_sem=up_recv.at[source, part],
+            device_id={"expert": peer},
+            device_id_type=MESH,
+        )
+
+    def spread_on(zs, part, op):
+        source = device(zs, col, core)
+        up_from = (zs <= z) & (z + 1 < depth)
+        down_from = (zs >= z) & (z >= 1)
+
+        @pl.when(up_from)
+        def _():
+            op(up_copy(source, part, zs, 0, device(jnp.minimum(z + 1, depth - 1), col, core)))
+
+        @pl.when(down_from)
+        def _():
+            op(up_copy(source, part, zs, 1, device(jnp.maximum(z - 1, 0), col, core)))
+
+        op(up_copy(source, part, zs, 2, device(z, 1 - col, core)))
+        op(up_copy(source, part, zs, 3, device(z, col, 1 - core)))
+
+    def across(zs, part, op):
+        op(up_copy(device(zs, 1 - col, core), part, zs, 4, device(z, col, 1 - core)))
+
+    def ordered(i):
+        low = jnp.minimum(z, depth - 1 - z)
+        middle = jnp.where(i == 0, 1, jnp.where(i == 1, 2, jnp.where(i == 2, 0, 3)))
+        near = jnp.where(low == 0, i, middle)
+        return jnp.where(z < 2, near, depth - 1 - near)
+
+    for part in range(CHUNKS):
+        spread_on(z, part, lambda copy: copy.start())
+
+    def block_copy(out, into, send, recv, peer):
+        return pltpu.make_async_remote_copy(
+            src_ref=out.at[peer],
+            dst_ref=into.at[me],
+            send_sem=send.at[peer],
+            recv_sem=recv.at[me],
+            device_id={"expert": peer},
+            device_id_type=MESH,
+        )
+
+    def arrival(out, into, send, recv, source):
+        return pltpu.make_async_remote_copy(
+            src_ref=out.at[source],
+            dst_ref=into.at[source],
+            send_sem=send.at[source],
+            recv_sem=recv.at[source],
+            device_id={"expert": source},
+            device_id_type=MESH,
+        )
+
+    meta_set = (meta_out, meta_in, meta_send, meta_recv)
+    inner_set = (inner_out, inner_in, inner_send, inner_recv)
+    ret_set = (ret_out, ret_in, ret_send, ret_recv)
+
+    @pl.loop(1, devs)
+    def _(i):
+        block_copy(*meta_set, lax.rem(me + i, devs)).start()
+
+    meta_in[me] = meta_out[me]
+
+    def send_pair(block_set, j):
+        out, into = block_set[0], block_set[1]
+        for c in range(2):
+            peer = j * 2 + c
+
+            @pl.when(peer != me)
+            def _():
+                block_copy(*block_set, peer).start()
+
+            @pl.when(peer == me)
+            def _():
+                into[me] = out[me]
+
+    @pl.loop(0, chips)
+    def _(i):
+        j = lax.rem(chip + chips // 2 + i, chips)
+        take = iota((2 * cap, slots), 0) + j * (2 * cap) == target_row[0:1, :]
+        packed = jnp.dot(
+            jnp.where(take, 1.0, 0.0).astype(bf16), inner[...], preferred_element_type=f32
+        )
+        inner_out[pl.ds(j * 2, 2)] = packed.astype(bf16).reshape(2, cap, hidden)
+        send_pair(inner_set, j)
+
+    total[...] = jnp.zeros_like(total)
+
+    def wait_pair(block_set, j):
+        for c in range(2):
+            source = j * 2 + c
+
+            @pl.when(source != me)
+            def _():
+                arrival(*block_set, source).wait_recv()
+
+    def wait_up(source):
+        for part in range(CHUNKS):
+            up_copy(source, part, 0, 0, device(z, col, 1 - core)).wait_recv()
+
+    def compute(zs, xs):
+        j = zs * 2 + xs
+        wait_up(device(zs, xs, 1 - core))
+        wait_pair(meta_set, j)
+        pair = pl.ds(j * 2, 2)
+        notes = meta_in[pair]
+        columns = jnp.concatenate([jnp.transpose(notes[0]), jnp.transpose(notes[1])], axis=0)
+        second = iota((2 * tok, 1), 0) >= tok
+        scale = columns[:, 0:1]
+        rank_col = (columns[:, 1:2] + jnp.where(second, float(cap), 0.0)).astype(i32)
+        rank_row = jnp.concatenate([notes[0][1:2], notes[1][1:2] + float(cap)], axis=1).astype(i32)
+        block = up_all[pair].reshape(2 * tok, up_all.shape[2])
+        weighted[...] = (scale * block.astype(f32)).astype(bf16)
+        slot_grad = jnp.dot(weighted[...], down[...], preferred_element_type=f32).astype(bf16)
+        pick = jnp.where(iota((2 * cap, 2 * tok), 0) == rank_row, 1.0, 0.0).astype(bf16)
+        packed = jnp.dot(pick, slot_grad, preferred_element_type=f32).astype(bf16)
+        ret_out[pair] = packed.reshape(2, cap, hidden)
+        send_pair(ret_set, j)
+        wait_pair(inner_set, j)
+        place = jnp.where(iota((2 * tok, 2 * cap), 1) == rank_col, 1.0, 0.0).astype(bf16)
+        rows_h = jnp.dot(
+            place, inner_in[pair].reshape(2 * cap, hidden), preferred_element_type=f32
+        ).astype(bf16)
+        total[...] += lax.dot_general(
+            weighted[...], rows_h, (((0,), (0,)), ((), ())), preferred_element_type=f32
+        )
+
+    @pl.loop(0, depth + 2)
+    def _(i):
+        @pl.when((i >= 1) & (i < depth))
+        def _():
+            zs = ordered(i)
+            for part in range(CHUNKS):
+                up_copy(device(zs, col, core), part, 0, 0, device(z, 1 - col, core)).wait_recv()
+                spread_on(zs, part, lambda copy: copy.start())
+
+        @pl.when((i >= 1) & (i < depth + 1))
+        def _():
+            zs = ordered(i - 1)
+            for part in range(CHUNKS):
+                up_copy(device(zs, 1 - col, core), part, 0, 0, device(z, 1 - col, core)).wait_recv()
+                across(zs, part, lambda copy: copy.start())
+
+        @pl.loop(0, 2)
+        def _(p):
+            lag = i - 1 - p
+
+            @pl.when((lag >= 0) & (lag < depth))
+            def _():
+                compute(ordered(lag), jnp.where(p == 0, col, 1 - col))
+
+    grad_down[...] = total[...].astype(bf16)
+
+    @pl.loop(1, devs)
+    def _(i):
+        arrival(*ret_set, lax.rem(me + i, devs)).wait_recv()
+
+    tile = 256
+
+    @pl.loop(0, slots // tile)
+    def _(i):
+        at = pl.ds(pl.multiple_of(i * tile, tile), tile)
+        put = iota((tile, devs * cap), 1) == target_col[at, 0:1]
+        grad_inner[at, :] = jnp.dot(
+            jnp.where(put, 1.0, 0.0).astype(bf16),
+            ret_in[...].reshape(devs * cap, hidden),
+            preferred_element_type=f32,
+        ).astype(bf16)
+
+    @pl.loop(1, devs)
+    def _(i):
+        peer = lax.rem(me + i, devs)
+        block_copy(*meta_set, peer).wait_send()
+        block_copy(*inner_set, peer).wait_send()
+        block_copy(*ret_set, peer).wait_send()
+
+    @pl.loop(0, depth)
+    def _(zs):
+        for part in range(CHUNKS):
+            spread_on(zs, part, lambda copy: copy.wait_send())
+            across(zs, part, lambda copy: copy.wait_send())
+
+
+def fused(inner, upstream, routes, gates, lengths, advantages, down_weight):
+    tok, top = routes.shape
+    width = upstream.shape[1]
+    hidden = inner.shape[2]
+    devs = lax.axis_size("expert")
+    slots = tok * top
+    cap = min(tok, max(2, 3 * slots // (2 * devs)))
+    bf16, f32, i32 = jnp.bfloat16, jnp.float32, jnp.int32
+    vmem = pl.BlockSpec(memory_space=pltpu.VMEM)
+    smem = pl.BlockSpec(memory_space=pltpu.SMEM)
+    dma = pltpu.SemaphoreType.DMA
+    flops = 4 * devs * tok * width * hidden
+    grad_inner, grad_down = pl.pallas_call(
+        functools.partial(kernel, devs, cap, lengths.shape[0]),
+        out_shape=(
+            jax.ShapeDtypeStruct((slots, hidden), bf16),
+            jax.ShapeDtypeStruct((width, hidden), bf16),
+        ),
+        in_specs=[vmem, vmem, vmem, smem, smem, vmem, pl.BlockSpec(memory_space=pl.ANY), vmem],
+        out_specs=(vmem, vmem),
+        scratch_shapes=[
+            pltpu.VMEM((devs, tok, width), bf16),
+            pltpu.VMEM((devs, 8, tok), f32),
+            pltpu.VMEM((devs, 8, tok), f32),
+            pltpu.VMEM((devs, cap, hidden), bf16),
+            pltpu.VMEM((devs, cap, hidden), bf16),
+            pltpu.VMEM((devs, cap, hidden), bf16),
+            pltpu.VMEM((devs, cap, hidden), bf16),
+            pltpu.VMEM((2 * tok, width), bf16),
+            pltpu.VMEM((width, hidden), f32),
+            pltpu.VMEM((8, slots), i32),
+            pltpu.VMEM((slots, 8), i32),
+            dma,
+            dma((devs // 4, 5, CHUNKS)),
+            dma((devs, CHUNKS)),
+            dma((devs,)),
+            dma((devs,)),
+            dma((devs,)),
+            dma((devs,)),
+            dma((devs,)),
+            dma((devs,)),
+        ],
+        compiler_params=pltpu.CompilerParams(
+            collective_id=0, has_side_effects=True, vmem_limit_bytes=48 * 1024 * 1024
+        ),
+        cost_estimate=pl.CostEstimate(flops=flops, bytes_accessed=8_000_000, transcendentals=0),
+    )(
+        routes.T,
+        gates.T,
+        routes.reshape(1, slots),
+        lengths,
+        advantages,
+        inner.reshape(slots, hidden),
+        upstream,
+        down_weight.reshape(width, hidden),
+    )
+    return grad_inner.reshape(tok, top, hidden), grad_down.reshape(1, width, hidden)
+
+
 def solution(mesh):
+    gathered = mesh.shape["dp"] == 1 and mesh.shape["expert"] == 16
+    body = fused if gathered else shards
     return jax.shard_map(
-        shards,
+        body,
         mesh=mesh,
         in_specs=(
             P(("groups", "dp", "expert"), None, None),

time: 238 us -> 106 us (0.45)
  waiting for transfers between devices: 143 us -> 0 us
  Pallas kernels: 0 us -> 96.3 us
  starting transfers between devices: 42.3 us -> 0 us
  other arithmetic: 19.5 us -> 0 us
  matrix products: 14.3 us -> 0 us
  local copies, waits for them, and re-layouts: 16.5 us -> 9.17 us
    all_to_all x3 -> x0, waiting for transfers between devices: 143 us -> none  [the longest x1 108 us: shards(): lax.all_to_all(send_w.reshape(expert_devs, block_rows, width), 'expert',...]
    pallas_call x0 -> x1, Pallas kernels: none -> 96.3 us  [fused(): pl.pallas_call(functools.partial(kernel, devs, cap, lengths.shape[0]), ou...]
    all_to_all x3 -> x0, starting transfers between devices: 42.3 us -> none  [the longest x1 27.7 us: shards(): lax.all_to_all(send_h.reshape(expert_devs, block_rows, hidden), 'expert',...]
    dot_general x2 -> x0, matrix products: 14.3 us -> none  [the longest x1 7.35 us: shards(): jnp.einsum('sect,eth->sech', columns, lax.all_gather(down_weight, 'dp', a...]
    scatter x1 -> x0, other arithmetic: 10.6 us -> none  [shards(): jnp.zeros((buffer_rows, width), jnp.bfloat16).at[target].set(flat_weighted)]
    scatter x1 -> x0, local copies, waits for them, and re-layouts: 6.13 us -> none  [shards(): jnp.zeros((buffer_rows, hidden), jnp.bfloat16).at[target].set(flat_inner)]
    another operation x4 -> x0, other arithmetic: 5.46 us -> none
    gather x1 -> x0, local copies, waits for them, and re-layouts: 4.99 us -> none  [shards(): grad_inner = grad_slots[target].reshape(tok_rows, top_count, hidden)]
  transfers between devices with their start and end apart: 3 -> 0, of which waited for: 3 -> 0; matrix products, arithmetic and copies ran while one was open for 10% -> 0% of each run, Pallas kernels for 0% -> 0%
where the time goes in v1:
time: 106 us
  Pallas kernels  96.3 us (91%)
  local copies, waits for them, and re-layouts  9.17 us (9%)
    pallas_call x1, Pallas kernels, fused(): pl.pallas_call(functools.partial(kernel, devs, cap, lengths.shape[0]), ou...  96.3 us
    unnamed x17, local copies, waits for them, and re-layouts  9.07 us

profile of v1, /device:TPU:1, one launch (start us, length us, event | category | flops | bytes accessed | tf_op | source)
XLA Modules:
  0.0 106.1 jit_solution(6481348592245849993)
XLA Ops:
  0.6 0.8 copy.10
  1.4 0.1 reshape.19.routes_row
  1.5 0.0 copy-start
  1.5 0.7 copy-done
  2.2 0.0 copy-start.1
  2.2 1.4 %copy-done.1 = bf16[1,2048,384]{2,1,0:T(8,128)(2,1)S(1)} copy-done((bf16[1,2048,384]{2,1,0:T(8,128)(2,1)S(1)}, bf16[1,2048,384]{2,1,0:T(8,128)(2,1)}, u32[]{:S(2)}) %copy-start.1) | copy-done | bytes 1572888
  3.6 0.0 copy-start.2
  3.6 1.1 %copy-done.2 = bf16[128,8,384]{2,1,0:T(8,128)(2,1)S(1)} copy-done((bf16[128,8,384]{2,1,0:T(8,128)(2,1)S(1)}, bf16[128,8,384]{2,1,0:T(8,128)(2,1)}, u32[]{:S(2)}) %copy-start.2) | copy-done | bytes 786456
  4.7 0.0 copy-start.3
  4.7 1.0 copy-done.3
  5.8 0.0 copy-start.4
  5.8 0.7 copy-done.4
  6.5 0.0 copy-start.5
  6.5 0.7 copy-done.5
  7.1 0.0 copy-start.6
  7.1 0.7 copy-done.6
  7.8 96.3 %shard_map.86 = (bf16[1024,384]{1,0:T(8,128)(2,1)S(1)}, bf16[2048,384]{1,0:T(8,128)(2,1)S(1)}) custom-call(s32[8,128]{1,0:T(8,128)S(1)} %bitcast.8, f32[8,128]{1,0:T(8,128)S(1)} %bitcast.11, s32[1,1024]{1,0:T(1,128)S(1)} %reshape.19.routes_row, s32[2]{0:T(128)S(1)} %copy-done.5, f32[2]{0:T(128)S(1)} %copy-done.6, bf16[1024,384]{1,0:T(8,128)(2,1)S(1)} %bitcast.10, ...), custom_call_target="tpu_custom_call" | custom-call | flops 6442450944 | bytes 8000000 | tf_op jit(solution)/shard_map/pallas_call | solution.py:396
  104.1 0.9 copy.13
  105.0 1.1 %copy.14 = bf16[1,2048,384]{2,1,0:T(8,128)(2,1)} copy(bf16[1,2048,384]{2,1,0:T(8,128)(2,1)S(1)} %bitcast.6) | data formatting | bytes 3145728
Async XLA Ops:
  1.5 0.7 copy-start
  2.2 1.4 %copy-start.1 = (bf16[1,2048,384]{2,1,0:T(8,128)(2,1)S(1)}, bf16[1,2048,384]{2,1,0:T(8,128)(2,1)}, u32[]{:S(2)}) copy-start(bf16[1,2048,384]{2,1,0:T(8,128)(2,1)} %param.13) | copy-start | bytes 4718596
  3.6 1.1 %copy-start.2 = (bf16[128,8,384]{2,1,0:T(8,128)(2,1)S(1)}, bf16[128,8,384]{2,1,0:T(8,128)(2,1)}, u32[]{:S(2)}) copy-start(bf16[128,8,384]{2,1,0:T(8,128)(2,1)} %param.7) | copy-start | bytes 2359300
  4.7 1.0 copy-start.3
  5.8 0.7 copy-start.4
  6.5 0.7 copy-start.5
  7.1 0.7 copy-start.6

commit v2 on v1

--- a/solution.py
+++ b/solution.py
@@ -87,21 +87,24 @@
 
 
 MESH = pl.DeviceIdType.MESH
-CHUNKS = 2
+CHUNKS = 4
+LATE = 3
+VMEM_BYTES = 64 * 1024 * 1024 - 64 * 1024
 
 
 def kernel(
     devs,
     cap,
     seqs,
-    routes_t,
-    gates_t,
-    routes_row,
-    lengths,
-    advantages,
-    inner,
+    routes_hbm,
+    gates_hbm,
+    lengths_hbm,
+    advantages_hbm,
+    inner_hbm,
     upstream,
-    down,
+    down_hbm,
+    grad_inner_hbm,
+    grad_down_hbm,
     grad_inner,
     grad_down,
     up_all,
@@ -115,7 +118,15 @@
     total,
     target_row,
     target_col,
+    routes,
+    gates,
+    lengths,
+    advantages,
+    inner,
+    down,
     own_sem,
+    stage_sem,
+    out_sem,
     up_send,
     up_recv,
     meta_send,
@@ -125,7 +136,7 @@
     ret_send,
     ret_recv,
 ):
-    top, tok = routes_t.shape
+    top, tok = routes.shape
     slots = top * tok
     hidden = down.shape[1]
     depth = devs // 4
@@ -146,6 +157,21 @@
 
     own = pltpu.make_async_copy(upstream, up_all.at[me], own_sem)
     own.start()
+    staged = [
+        pltpu.make_async_copy(far, near, stage_sem.at[i])
+        for i, (far, near) in enumerate(
+            (
+                (routes_hbm, routes),
+                (gates_hbm, gates),
+                (lengths_hbm, lengths),
+                (advantages_hbm, advantages),
+                (inner_hbm, inner),
+                (down_hbm, down),
+            )
+        )
+    ]
+    for copy in staged:
+        copy.start()
     barrier = pltpu.get_barrier_semaphore()
 
     @pl.loop(1, devs)
@@ -153,7 +179,51 @@
         peer = lax.rem(me + i, devs)
         pl.semaphore_signal(barrier, inc=1, device_id={"expert": peer}, device_id_type=MESH)
 
-    routed = routes_t[...]
+    own.wait()
+    pl.semaphore_wait(barrier, devs - 1)
+
+    def up_copy(source, part, zs, kind, peer):
+        block = up_all.at[source, pl.ds(part * rows, rows)]
+        return pltpu.make_async_remote_copy(
+            src_ref=block,
+            dst_ref=block,
+            send_sem=up_send.at[zs, kind, part],
+            recv_sem=up_recv.at[source, part],
+            device_id={"expert": peer},
+            device_id_type=MESH,
+        )
+
+    def spread_on(zs, part, op):
+        source = device(zs, col, core)
+        up_from = (zs <= z) & (z + 1 < depth)
+        down_from = (zs >= z) & (z >= 1)
+
+        @pl.when(up_from)
+        def _():
+            op(up_copy(source, part, zs, 0, device(jnp.minimum(z + 1, depth - 1), col, core)))
+
+        @pl.when(down_from)
+        def _():
+            op(up_copy(source, part, zs, 1, device(jnp.maximum(z - 1, 0), col, core)))
+
+        op(up_copy(source, part, zs, 2, device(z, 1 - col, core)))
+        op(up_copy(source, part, zs, 3, device(z, col, 1 - core)))
+
+    def across(zs, part, op):
+        op(up_copy(device(zs, 1 - col, core), part, zs, 4, device(z, col, 1 - core)))
+
+    def ordered(i):
+        low = jnp.minimum(z, depth - 1 - z)
+        middle = jnp.where(i == 0, 1, jnp.where(i == 1, 2, jnp.where(i == 2, 0, 3)))
+        near = jnp.where(low == 0, i, middle)
+        return jnp.where(z < 2, near, depth - 1 - near)
+
+    for part in range(CHUNKS):
+        spread_on(z, part, lambda copy: copy.start())
+
+    for copy in staged[:4]:
+        copy.wait()
+    routed = routes[...]
     position = me * tok + iota((1, tok), 1)
     token_adv = jnp.zeros((1, tok), f32)
     first = jnp.int32(0)
@@ -162,7 +232,7 @@
         held = (position >= first) & (position < last)
         token_adv = jnp.where(held, advantages[s], token_adv)
         first = last
-    factor = gates_t[...] * token_adv
+    factor = gates[...] * token_adv
     named, factors = [], []
     for e in range(devs):
         hit = routed == e
@@ -180,56 +250,19 @@
     lane, row = iota((tok, slots), 1), iota((tok, slots), 0)
     spread = jnp.where((lane >= row * top) & (lane < (row + 1) * top), 1.0, 0.0).astype(bf16)
     by_slot = jnp.dot(rank.astype(bf16), spread, preferred_element_type=f32)
+    place_in = iota((top, slots), 1) & (top - 1)
+    repeated = jnp.dot(routed.astype(f32).astype(bf16), spread, preferred_element_type=f32)
+    routes_row = jnp.sum(
+        jnp.where(place_in == iota((top, slots), 0), repeated, 0.0), axis=0, keepdims=True
+    ).astype(i32)
     which = iota((devs, slots), 0)
     start_of = (which * cap).astype(f32)
     aim = jnp.sum(
-        jnp.where(which == routes_row[...], by_slot + start_of, 0.0), axis=0, keepdims=True
+        jnp.where(which == routes_row, by_slot + start_of, 0.0), axis=0, keepdims=True
     )
     aim8 = jnp.broadcast_to(aim, (8, slots))
     target_row[...] = aim8.astype(i32)
     target_col[...] = jnp.transpose(aim8).astype(i32)
-
-    own.wait()
-    pl.semaphore_wait(barrier, devs - 1)
-
-    def up_copy(source, part, zs, kind, peer):
-        block = up_all.at[source, pl.ds(part * rows, rows)]
-        return pltpu.make_async_remote_copy(
-            src_ref=block,
-            dst_ref=block,
-            send_sem=up_send.at[zs, kind, part],
-            recv_sem=up_recv.at[source, part],
-            device_id={"expert": peer},
-            device_id_type=MESH,
-        )
-
-    def spread_on(zs, part, op):
-        source = device(zs, col, core)
-        up_from = (zs <= z) & (z + 1 < depth)
-        down_from = (zs >= z) & (z >= 1)
-
-        @pl.when(up_from)
-        def _():
-            op(up_copy(source, part, zs, 0, device(jnp.minimum(z + 1, depth - 1), col, core)))
-
-        @pl.when(down_from)
-        def _():
-            op(up_copy(source, part, zs, 1, device(jnp.maximum(z - 1, 0), col, core)))
-
-        op(up_copy(source, part, zs, 2, device(z, 1 - col, core)))
-        op(up_copy(source, part, zs, 3, device(z, col, 1 - core)))
-
-    def across(zs, part, op):
-        op(up_copy(device(zs, 1 - col, core), part, zs, 4, device(z, col, 1 - core)))
-
-    def ordered(i):
-        low = jnp.minimum(z, depth - 1 - z)
-        middle = jnp.where(i == 0, 1, jnp.where(i == 1, 2, jnp.where(i == 2, 0, 3)))
-        near = jnp.where(low == 0, i, middle)
-        return jnp.where(z < 2, near, depth - 1 - near)
-
-    for part in range(CHUNKS):
-        spread_on(z, part, lambda copy: copy.start())
 
     def block_copy(out, into, send, recv, peer):
         return pltpu.make_async_remote_copy(
@@ -274,17 +307,25 @@
             def _():
                 into[me] = out[me]
 
+    staged[4].wait()
+
     @pl.loop(0, chips)
     def _(i):
-        j = lax.rem(chip + chips // 2 + i, chips)
+        zs = lax.rem(z + i + 1, depth)
+        xs = jnp.where(i < depth, col, 1 - col)
+        j = zs * 2 + xs
         take = iota((2 * cap, slots), 0) + j * (2 * cap) == target_row[0:1, :]
         packed = jnp.dot(
             jnp.where(take, 1.0, 0.0).astype(bf16), inner[...], preferred_element_type=f32
         )
         inner_out[pl.ds(j * 2, 2)] = packed.astype(bf16).reshape(2, cap, hidden)
-        send_pair(inner_set, j)
+
+        @pl.when(xs == col)
+        def _():
+            send_pair(inner_set, j)
 
     total[...] = jnp.zeros_like(total)
+    staged[5].wait()
 
     def wait_pair(block_set, j):
         for c in range(2):
@@ -305,36 +346,53 @@
         pair = pl.ds(j * 2, 2)
         notes = meta_in[pair]
         columns = jnp.concatenate([jnp.transpose(notes[0]), jnp.transpose(notes[1])], axis=0)
-        second = iota((2 * tok, 1), 0) >= tok
         scale = columns[:, 0:1]
-        rank_col = (columns[:, 1:2] + jnp.where(second, float(cap), 0.0)).astype(i32)
         rank_row = jnp.concatenate([notes[0][1:2], notes[1][1:2] + float(cap)], axis=1).astype(i32)
         block = up_all[pair].reshape(2 * tok, up_all.shape[2])
-        weighted[...] = (scale * block.astype(f32)).astype(bf16)
-        slot_grad = jnp.dot(weighted[...], down[...], preferred_element_type=f32).astype(bf16)
+        weighted[j] = (scale * block.astype(f32)).astype(bf16)
+        slot_grad = jnp.dot(weighted[j], down[...], preferred_element_type=f32).astype(bf16)
         pick = jnp.where(iota((2 * cap, 2 * tok), 0) == rank_row, 1.0, 0.0).astype(bf16)
         packed = jnp.dot(pick, slot_grad, preferred_element_type=f32).astype(bf16)
         ret_out[pair] = packed.reshape(2, cap, hidden)
         send_pair(ret_set, j)
+
+    def add_up(j):
         wait_pair(inner_set, j)
+        pair = pl.ds(j * 2, 2)
+        notes = meta_in[pair]
+        ranks = jnp.concatenate([jnp.transpose(notes[0]), jnp.transpose(notes[1])], axis=0)
+        second = iota((2 * tok, 1), 0) >= tok
+        rank_col = (ranks[:, 1:2] + jnp.where(second, float(cap), 0.0)).astype(i32)
         place = jnp.where(iota((2 * tok, 2 * cap), 1) == rank_col, 1.0, 0.0).astype(bf16)
         rows_h = jnp.dot(
             place, inner_in[pair].reshape(2 * cap, hidden), preferred_element_type=f32
         ).astype(bf16)
         total[...] += lax.dot_general(
-            weighted[...], rows_h, (((0,), (0,)), ((), ())), preferred_element_type=f32
-        )
-
-    @pl.loop(0, depth + 2)
-    def _(i):
-        @pl.when((i >= 1) & (i < depth))
+            weighted[j], rows_h, (((0,), (0,)), ((), ())), preferred_element_type=f32
+        )
+
+    outer = (z == 0) | (z == depth - 1)
+
+    @pl.loop(1, depth + 2)
+    def _(i):
+        @pl.loop(0, 2)
+        def _(q):
+            number = jnp.where(outer, i, i + jnp.where(i == 1, q, 1))
+
+            @pl.when((number < depth) & ((q == 0) | ((i == 1) & jnp.logical_not(outer))))
+            def _():
+                zs = ordered(number)
+                for part in range(CHUNKS):
+                    up_copy(device(zs, col, core), part, 0, 0, device(z, 1 - col, core)).wait_recv()
+                    spread_on(zs, part, lambda copy: copy.start())
+
+        @pl.when(i == LATE)
         def _():
-            zs = ordered(i)
-            for part in range(CHUNKS):
-                up_copy(device(zs, col, core), part, 0, 0, device(z, 1 - col, core)).wait_recv()
-                spread_on(zs, part, lambda copy: copy.start())
-
-        @pl.when((i >= 1) & (i < depth + 1))
+            @pl.loop(0, depth)
+            def _(step):
+                send_pair(inner_set, lax.rem(z + step + 1, depth) * 2 + 1 - col)
+
+        @pl.when(i < depth + 1)
         def _():
             zs = ordered(i - 1)
             for part in range(CHUNKS):
@@ -349,13 +407,23 @@
             def _():
                 compute(ordered(lag), jnp.where(p == 0, col, 1 - col))
 
+    @pl.loop(0, chips)
+    def _(i):
+        add_up(ordered(lax.rem(i, depth)) * 2 + jnp.where(i < depth, col, 1 - col))
+
     grad_down[...] = total[...].astype(bf16)
+    down_out = pltpu.make_async_copy(grad_down, grad_down_hbm, out_sem.at[0])
+    down_out.start()
 
     @pl.loop(1, devs)
     def _(i):
         arrival(*ret_set, lax.rem(me + i, devs)).wait_recv()
 
     tile = 256
+
+    def tile_out(i):
+        at = pl.ds(pl.multiple_of(i * tile, tile), tile)
+        return pltpu.make_async_copy(grad_inner.at[at], grad_inner_hbm.at[at], out_sem.at[1 + i])
 
     @pl.loop(0, slots // tile)
     def _(i):
@@ -366,6 +434,7 @@
             ret_in[...].reshape(devs * cap, hidden),
             preferred_element_type=f32,
         ).astype(bf16)
+        tile_out(i).start()
 
     @pl.loop(1, devs)
     def _(i):
@@ -379,6 +448,12 @@
         for part in range(CHUNKS):
             spread_on(zs, part, lambda copy: copy.wait_send())
             across(zs, part, lambda copy: copy.wait_send())
+
+    down_out.wait()
+
+    @pl.loop(0, slots // tile)
+    def _(i):
+        tile_out(i).wait()
 
 
 def fused(inner, upstream, routes, gates, lengths, advantages, down_weight):
@@ -389,8 +464,7 @@
     slots = tok * top
     cap = min(tok, max(2, 3 * slots // (2 * devs)))
     bf16, f32, i32 = jnp.bfloat16, jnp.float32, jnp.int32
-    vmem = pl.BlockSpec(memory_space=pltpu.VMEM)
-    smem = pl.BlockSpec(memory_space=pltpu.SMEM)
+    hbm = pl.BlockSpec(memory_space=pltpu.HBM)
     dma = pltpu.SemaphoreType.DMA
     flops = 4 * devs * tok * width * hidden
     grad_inner, grad_down = pl.pallas_call(
@@ -399,9 +473,11 @@
             jax.ShapeDtypeStruct((slots, hidden), bf16),
             jax.ShapeDtypeStruct((width, hidden), bf16),
         ),
-        in_specs=[vmem, vmem, vmem, smem, smem, vmem, pl.BlockSpec(memory_space=pl.ANY), vmem],
-        out_specs=(vmem, vmem),
+        in_specs=[hbm] * 7,
+        out_specs=(hbm, hbm),
         scratch_shapes=[
+            pltpu.VMEM((slots, hidden), bf16),
+            pltpu.VMEM((width, hidden), bf16),
             pltpu.VMEM((devs, tok, width), bf16),
             pltpu.VMEM((devs, 8, tok), f32),
             pltpu.VMEM((devs, 8, tok), f32),
@@ -409,11 +485,19 @@
             pltpu.VMEM((devs, cap, hidden), bf16),
             pltpu.VMEM((devs, cap, hidden), bf16),
             pltpu.VMEM((devs, cap, hidden), bf16),
-            pltpu.VMEM((2 * tok, width), bf16),
+            pltpu.VMEM((devs // 2, 2 * tok, width), bf16),
             pltpu.VMEM((width, hidden), f32),
             pltpu.VMEM((8, slots), i32),
             pltpu.VMEM((slots, 8), i32),
+            pltpu.VMEM((top, tok), i32),
+            pltpu.VMEM((top, tok), f32),
+            pltpu.SMEM(lengths.shape, i32),
+            pltpu.SMEM(advantages.shape, f32),
+            pltpu.VMEM((slots, hidden), bf16),
+            pltpu.VMEM((width, hidden), bf16),
             dma,
+            dma((6,)),
+            dma((1 + slots // 256,)),
             dma((devs // 4, 5, CHUNKS)),
             dma((devs, CHUNKS)),
             dma((devs,)),
@@ -424,13 +508,12 @@
             dma((devs,)),
         ],
         compiler_params=pltpu.CompilerParams(
-            collective_id=0, has_side_effects=True, vmem_limit_bytes=48 * 1024 * 1024
+            collective_id=0, has_side_effects=True, vmem_limit_bytes=VMEM_BYTES
         ),
         cost_estimate=pl.CostEstimate(flops=flops, bytes_accessed=8_000_000, transcendentals=0),
     )(
         routes.T,
         gates.T,
-        routes.reshape(1, slots),
         lengths,
         advantages,
         inner.reshape(slots, hidden),
@@ -438,7 +521,6 @@
         down_weight.reshape(width, hidden),
     )
     return grad_inner.reshape(tok, top, hidden), grad_down.reshape(1, width, hidden)
-
 
 def solution(mesh):
     gathered = mesh.shape["dp"] == 1 and mesh.shape["expert"] == 16

time: 106 us -> 95.4 us (0.900)
  local copies, waits for them, and re-layouts: 9.17 us -> 3.36 us
  Pallas kernels: 96.3 us -> 91.2 us
    unnamed x17 -> x4, local copies, waits for them, and re-layouts: 9.07 us -> 3.36 us
    pallas_call x1, Pallas kernels: 96.3 us -> 91.2 us  [fused(): pl.pallas_call(functools.partial(kernel, devs, cap, lengths.shape[0]), ou...]
where the time goes in v2:
time: 95.4 us; the launch traced here: 95.2 us
  Pallas kernels  91.2 us (96%)
  local copies, waits for them, and re-layouts  3.36 us (4%)
    pallas_call x1, Pallas kernels, fused(): pl.pallas_call(functools.partial(kernel, devs, cap, lengths.shape[0]), ou...  91.2 us
    unnamed x4, local copies, waits for them, and re-layouts  3.36 us

profile of v2, /device:TPU:1, one launch (start us, length us, event | category | flops | bytes accessed | tf_op | source)
XLA Modules:
  0.0 95.2 jit_solution(1251207310716370751)
XLA Ops:
  0.6 91.2 %shard_map.86 = (bf16[1024,384]{1,0:T(8,128)(2,1)}, bf16[2048,384]{1,0:T(8,128)(2,1)}) custom-call(s32[8,128]{1,0:T(8,128)} %bitcast.10, f32[8,128]{1,0:T(8,128)} %bitcast.11, s32[2]{0:T(128)} %lengths_hbm.1, f32[2]{0:T(128)} %advantages_hbm.1, bf16[1024,384]{1,0:T(8,128)(2,1)} %bitcast.9, bf16[128,2048]{1,0:T(8,128)(2,1)} %upstream.1, bf16[2048,384]{1,0:T(8,128)(2,1)} %bitcast.8), custom_call_target="tpu_custom_call" | custom-call | flops 6442450944 | bytes 8000000 | tf_op jit(solution)/shard_map/pallas_call | solution.py:470
  91.8 0.0 copy-start
  91.8 2.2 %copy.11 = bf16[128,8,384]{2,1,0:T(8,128)(2,1)} copy(bf16[128,8,384]{2,1,0:T(8,128)(2,1)} %bitcast.7) | data formatting | bytes 1572864
  94.0 0.0 copy-done
  94.0 1.1 %copy.12 = bf16[1,2048,384]{2,1,0:T(8,128)(2,1)} copy(bf16[1,2048,384]{2,1,0:T(8,128)(2,1)S(1)} %bitcast.6) | data formatting | bytes 3145728
Async XLA Ops:
  91.8 2.2 %copy-start = (bf16[2048,384]{1,0:T(8,128)(2,1)S(1)}, bf16[2048,384]{1,0:T(8,128)(2,1)}, u32[]{:S(2)}) copy-start(bf16[2048,384]{1,0:T(8,128)(2,1)} %get-tuple-element.5) | copy-start | bytes 4718596
